TPU v7x, 32 devices: a whole 2x2x4 slice. The times are simulated.
32 devices in a mesh: parts: 2 (over x), dp: 2 (over core), tensor: 8 (over z, y).
Axes of the slice: x: 2, y: 2, z: 4, core: 2. Of those that a mesh axis runs over, the one named last changes fastest.
Arguments:
- tokens: bfloat16 [2048, 8192], P(('parts', 'dp'), 'tensor'), parts along dimension 0, may hold values from -6 to 6
- cotangent: bfloat16 [2048, 8192], P(('parts', 'dp'), 'tensor'), parts along dimension 0, may hold values from -6 to 6
- gate_weight: bfloat16 [8192, 14336], P('dp', 'tensor'), may hold values from -0.0625 to 0.0625
- up_weight: bfloat16 [8192, 14336], P('dp', 'tensor'), may hold values from -0.0625 to 0.0625
- down_weight: bfloat16 [14336, 8192], P('tensor', 'dp'), may hold values from -0.0625 to 0.0625
- proj_tokens: bfloat16 [8192, 64], P('tensor'), may hold values from -0.0625 to 0.0625
- proj_cotangent: bfloat16 [8192, 64], P('tensor'), may hold values from -0.0625 to 0.0625
- proj_hidden: bfloat16 [14336, 64], P('tensor'), may hold values from -0.046875 to 0.046875
- proj_gate: bfloat16 [14336, 64], P('tensor'), may hold values from -0.046875 to 0.046875
- proj_up: bfloat16 [14336, 64], P('tensor'), may hold values from -0.046875 to 0.046875
- doc_ids: int32 [4, 512], P(('parts', 'dp')), parts along dimension 0, may hold values from 0 to 7, never falling along the last dimension, each value on 1 to 256 neighbouring positions
- query_grads: bfloat16 [512, 12288], P('tensor'), may hold values from -0.029907227 to 0.029907227
Outputs:
- scores: float32 [32, 512], P(('parts', 'dp'), 'tensor'), parts along dimension 0
There are 2 independent parts, one for each index of `parts`. A program takes and returns all parts, laid end to end along the dimension named above; an argument that names none is the same for every part. Nothing has to cross between parts.
Inputs may be any that keep to these rules, and one draw needn't show every extreme that they name: `doc_ids`: within each group the ids never fall; every id names 1 to 256 rows, and one names exactly 256.
All inputs are finite; a program needn't handle non-finite values.
Results may differ from a plain program's by a relative error of at most 0.0028.
Values may be sent and summed in bfloat16 or wider, within the bound.
A program may use at most 320 MiB of HBM per device.

v0:
```python
import jax
import jax.numpy as jnp
from jax import lax
from jax.sharding import PartitionSpec as P

RANK = 64
DOCS = 8


def outer_sums(onehot, left, right):
    weighted = (onehot[:, :, None] * left[:, None, :]).reshape(left.shape[0], -1)
    block = lax.dot_general(
        weighted,
        right,
        (((0,), (0,)), ((), ())),
        precision=lax.Precision.HIGHEST,
        preferred_element_type=jnp.float32,
    )
    return block.reshape(onehot.shape[1], -1)


def group_factors(projected, doc_rows):
    onehot = (doc_rows[:, None] == jnp.arange(DOCS, dtype=jnp.int32)[None, :]).astype(jnp.float32)
    p_tokens = projected[:, 0:RANK]
    p_cotan = projected[:, RANK : 2 * RANK]
    p_hidden = projected[:, 2 * RANK : 3 * RANK]
    p_gate = projected[:, 3 * RANK : 4 * RANK]
    p_upgrad = projected[:, 4 * RANK : 5 * RANK]
    return jnp.concatenate(
        [
            outer_sums(onehot, p_gate, p_tokens),
            outer_sums(onehot, p_upgrad, p_tokens),
            outer_sums(onehot, p_cotan, p_hidden),
        ],
        axis=1,
    )


def local(
    tokens,
    cotangent,
    gate_weight,
    up_weight,
    down_weight,
    proj_tokens,
    proj_cotangent,
    proj_hidden,
    proj_gate,
    proj_up,
    doc_ids,
    query_grads,
):
    full_tokens, full_cotan = (
        lax.all_gather(tokens, "tensor", axis=1, tiled=True),
        lax.all_gather(cotangent, "tensor", axis=1, tiled=True),
    )
    columns = full_tokens
    gate_pre = jnp.dot(
        columns,
        lax.all_gather(gate_weight, "dp", axis=0, tiled=True),
        preferred_element_type=jnp.float32,
    )
    up_pre = jnp.dot(
        columns,
        lax.all_gather(up_weight, "dp", axis=0, tiled=True),
        preferred_element_type=jnp.float32,
    )
    columns = full_cotan
    grad_hidden = lax.dot_general(
        columns,
        lax.all_gather(down_weight, "dp", axis=1, tiled=True),
        (((1,), (1,)), ((), ())),
        preferred_element_type=jnp.float32,
    )
    sigmoid_gate = jax.nn.sigmoid(gate_pre)
    hidden = (gate_pre * sigmoid_gate * up_pre).astype(jnp.bfloat16)
    grad_up = (grad_hidden * gate_pre * sigmoid_gate).astype(jnp.bfloat16)
    grad_gate = (
        grad_hidden * up_pre * sigmoid_gate * (1.0 + gate_pre * (1.0 - sigmoid_gate))
    ).astype(jnp.bfloat16)
    stacked = jnp.concatenate(
        [
            jnp.dot(tokens, proj_tokens, preferred_element_type=jnp.float32),
            jnp.dot(cotangent, proj_cotangent, preferred_element_type=jnp.float32),
            jnp.dot(hidden, proj_hidden, preferred_element_type=jnp.float32),
            jnp.dot(grad_gate, proj_gate, preferred_element_type=jnp.float32),
            jnp.dot(grad_up, proj_up, preferred_element_type=jnp.float32),
        ],
        axis=1,
    )
    summed = lax.psum(stacked, "tensor")
    factors = group_factors(summed, doc_ids[0])
    return jnp.dot(
        factors,
        query_grads.astype(jnp.float32).T,
        precision=lax.Precision.HIGHEST,
        preferred_element_type=jnp.float32,
    )


def solution(mesh):
    return jax.shard_map(
        local,
        mesh=mesh,
        in_specs=(
            P(("parts", "dp"), "tensor"),
            P(("parts", "dp"), "tensor"),
            P("dp", "tensor"),
            P("dp", "tensor"),
            P("tensor", "dp"),
            P("tensor", None),
            P("tensor", None),
            P("tensor", None),
            P("tensor", None),
            P("tensor", None),
            P(("parts", "dp"), None),
            P("tensor", None),
        ),
        out_specs=P(("parts", "dp"), "tensor"),
        check_vma=False,
    )
```

profile of v0, /device:TPU:13, one launch (start us, length us, event | category | flops | bytes accessed | tf_op | source)
XLA Modules:
  0.0 528.9 jit_solution(5860941229087032251)
XLA Ops:
  6.5 0.7 all-gather.6.cloned.1.call-update
  7.3 0.7 all-gather.8.cloned.1.call-update
  8.1 0.7 all-gather.10.cloned.1.call-update
  8.8 0.5 all-gather.12.cloned.1.call-update
  9.4 0.5 all-gather.14.cloned.1.call-update
  10.0 0.6 copy-done.1
  10.5 0.4 convolution_dynamic-update-slice_fusion.1
  11.0 1.7 convolution_dynamic-update-slice_fusion
  12.7 119.9 %all-gather.6.cloned.1.call-done = bf16[512,8192]{1,0:T(8,128)(2,1)} async-done(((bf16[512,1024]{1,0:T(8,128)(2,1)}), bf16[512,8192]{1,0:T(8,128)(2,1)}) %all-gather.6.cloned.1.call-update) | async-done | bytes 8388624 | tf_op jit(solution)/shard_map/all_gather | solution.py:54
  132.5 50.4 %all-gather.8.cloned.1.call-done = bf16[8192,1792]{1,0:T(8,128)(2,1)} async-done(((bf16[4096,1792]{1,0:T(8,128)(2,1)}), bf16[8192,1792]{1,0:T(8,128)(2,1)}) %all-gather.8.cloned.1.call-update) | async-done | bytes 29360144 | tf_op jit(solution)/shard_map/all_gather | solution.py:60
  182.9 26.2 %fusion.24 = f32[512,1792]{1,0:T(8,128)} fusion(bf16[512,8192]{1,0:T(8,128)(2,1)} %all-gather.6.cloned.1.call-done, bf16[8192,1792]{1,0:T(8,128)(2,1)} %all-gather.8.cloned.1.call-done), kind=kOutput, calls=%fused_computation.34 | convolution fusion | flops 15032385536 | bytes 41418752 | tf_op jit(solution)/shard_map/dot_general | solution.py:58
  209.2 23.4 %all-gather.10.cloned.1.call-done = bf16[8192,1792]{1,0:T(8,128)(2,1)} async-done(((bf16[4096,1792]{1,0:T(8,128)(2,1)}), bf16[8192,1792]{1,0:T(8,128)(2,1)}) %all-gather.10.cloned.1.call-update) | async-done | bytes 29360144 | tf_op jit(solution)/shard_map/all_gather | solution.py:65
  232.5 21.1 %fusion.25 = f32[512,1792]{1,0:T(8,128)S(1)} fusion(bf16[512,8192]{1,0:T(8,128)(2,1)} %all-gather.6.cloned.1.call-done, bf16[8192,1792]{1,0:T(8,128)(2,1)} %all-gather.10.cloned.1.call-done), kind=kOutput, calls=%fused_computation.35 | convolution fusion | flops 15032385536 | bytes 41418752 | tf_op jit(solution)/shard_map/dot_general | solution.py:63
  253.7 1.8 copy-done.12
  255.5 1.3 fusion.5
  256.7 100.1 %all-gather.12.cloned.1.call-done = bf16[512,8192]{1,0:T(8,128)(2,1)} async-done(((bf16[512,1024]{1,0:T(8,128)(2,1)}), bf16[512,8192]{1,0:T(8,128)(2,1)}) %all-gather.12.cloned.1.call-update) | async-done | bytes 8388624 | tf_op jit(solution)/shard_map/all_gather | solution.py:55
  356.9 50.2 %all-gather.14.cloned.1.call-done = bf16[1792,8192]{1,0:T(8,128)(2,1)} async-done(((bf16[1792,4096]{1,0:T(8,128)(2,1)}), bf16[1792,8192]{1,0:T(8,128)(2,1)}) %all-gather.14.cloned.1.call-update) | async-done | bytes 29360144 | tf_op jit(solution)/shard_map/all_gather | solution.py:71
  407.1 22.8 %fusion.26 = f32[512,1792]{1,0:T(8,128)} fusion(bf16[512,8192]{1,0:T(8,128)(2,1)} %all-gather.12.cloned.1.call-done, bf16[1792,8192]{1,0:T(8,128)(2,1)} %all-gather.14.cloned.1.call-done), kind=kOutput, calls=%fused_computation.36 | convolution fusion | flops 15032385536 | bytes 41418752 | tf_op jit(solution)/shard_map/dot_general | solution.py:69
  429.9 5.9 %fusion.3 = f32[512,320]{0,1:T(8,128)S(1)} fusion(f32[512,320]{0,1:T(8,128)S(1)} %fusion.5, bf16[1792,64]{0,1:T(8,128)(2,1)S(1)} %copy-done.8, f32[512,1792]{1,0:T(8,128)} %fusion.24, f32[512,1792]{1,0:T(8,128)} %fusion.26, f32[512,1792]{1,0:T(8,128)} %copy-done.12), kind=kOutput, calls=%fused_computation.9 | convolution fusion | flops 126615552 | bytes 11370496 | tf_op jit(solution)/shard_map/dot_general | solution.py:86
  435.8 0.6 copy-done.13
  436.4 1.2 fusion.4
  437.6 0.8 copy-done.2
  438.5 72.4 %all-reduce.2.cloned.1.call-done = f32[512,320]{0,1:T(8,128)} async-done(((f32[512,320]{0,1:T(8,128)}), f32[512,320]{0,1:T(8,128)}) %all-reduce.2.cloned.1.call-update) | async-done | bytes 655376 | tf_op jit(solution)/shard_map/psum | solution.py:91
  510.9 1.1 fusion.23
  512.1 1.3 broadcast_multiply_fusion.2
  513.4 1.0 fusion.16
  514.3 0.8 reshape.49
  515.1 2.2 fusion.14
  517.3 0.8 reshape.50
  518.1 1.0 fusion.12
  519.0 0.1 reshape.51
  519.2 2.9 fusion.6
  (32 shorter events, 0.3 us)
Async XLA Ops:
  6.5 512.6 %copy-start = (bf16[64,12288]{1,0:T(8,128)(2,1)S(1)}, bf16[64,12288]{1,0:T(8,128)(2,1)}, u32[]{:S(2)}) copy-start(bf16[64,12288]{1,0:T(8,128)(2,1)} %param.23) | copy-start | bytes 4718596
  6.5 126.0 %all-gather.6.cloned.1.call-start = ((), (), s32[]{:S(2)}) async-start(), calls=%async_computation | async-start | bytes 9437184 | tf_op jit(solution)/shard_map/all_gather | solution.py:54
  7.3 175.7 %all-gather.8.cloned.1.call-start = ((), (), s32[]{:S(2)}) async-start(), calls=%async_computation.1 | async-start | bytes 44040192 | tf_op jit(solution)/shard_map/all_gather | solution.py:60
  8.0 224.5 %all-gather.10.cloned.1.call-start = ((), (), s32[]{:S(2)}) async-start(), calls=%async_computation.2 | async-start | bytes 44040192 | tf_op jit(solution)/shard_map/all_gather | solution.py:65
  8.7 348.1 %all-gather.12.cloned.1.call-start = ((), (), s32[]{:S(2)}) async-start(), calls=%async_computation.3 | async-start | bytes 9437184 | tf_op jit(solution)/shard_map/all_gather | solution.py:55
  9.3 1.2 copy-start.1
  9.3 1.2 copy-start.4
  9.3 1.7 copy-start.5
  9.3 397.8 %all-gather.14.cloned.1.call-start = ((), (), s32[]{:S(2)}) async-start(), calls=%async_computation.4 | async-start | bytes 44040192 | tf_op jit(solution)/shard_map/all_gather | solution.py:71
  9.9 501.0 %all-reduce.2.cloned.1.call-start = ((), (), s32[]{:S(2)}) async-start(), calls=%async_computation.5 | async-start | bytes 1310720 | tf_op jit(solution)/shard_map/psum | solution.py:91
  209.2 46.3 %copy-start.7 = (bf16[1792,64]{0,1:T(8,128)(2,1)S(1)}, bf16[1792,64]{0,1:T(8,128)(2,1)}, u32[]{:S(2)}) copy-start(bf16[1792,64]{0,1:T(8,128)(2,1)} %param.19) | copy-start | bytes 688132
  232.5 22.9 %copy-start.10 = (f32[512,1792]{1,0:T(8,128)S(1)}, f32[512,1792]{1,0:T(8,128)}, u32[]{:S(2)}) copy-start(f32[512,1792]{1,0:T(8,128)} %fusion.24) | copy-start | bytes 11010052
  253.7 1.8 copy-start.12
  256.7 173.2 %copy-start.8 = (bf16[1792,64]{0,1:T(8,128)(2,1)S(1)}, bf16[1792,64]{0,1:T(8,128)(2,1)}, u32[]{:S(2)}) copy-start(bf16[1792,64]{0,1:T(8,128)(2,1)} %param.20) | copy-start | bytes 688132
  429.9 5.9 %copy-start.9 = (bf16[1792,64]{0,1:T(8,128)(2,1)S(1)}, bf16[1792,64]{0,1:T(8,128)(2,1)}, u32[]{:S(2)}) copy-start(bf16[1792,64]{0,1:T(8,128)(2,1)} %param.21) | copy-start | bytes 688132
  429.9 5.9 %copy-start.11 = (f32[512,1792]{1,0:T(8,128)S(1)}, f32[512,1792]{1,0:T(8,128)}, u32[]{:S(2)}) copy-start(f32[512,1792]{1,0:T(8,128)} %fusion.24) | copy-start | bytes 11010052
  429.9 6.5 %copy-start.13 = (f32[512,1792]{1,0:T(8,128)S(1)}, f32[512,1792]{1,0:T(8,128)}, u32[]{:S(2)}) copy-start(f32[512,1792]{1,0:T(8,128)} %fusion.26) | copy-start | bytes 11010052
  436.4 2.1 copy-start.6
  437.6 0.9 copy-start.2
  510.9 2.4 copy-start.3
Sparse Core Ops, SparseCore 0:
  9.5 122.9 all-gather.5
  134.1 48.7 all-gather.7
  184.5 47.9 all-gather.9
  234.6 122.2 all-gather.11
  358.3 48.7 all-gather.13
  438.6 72.2 all-reduce.1
where the time goes:
time: 532 us; the launch traced here: 529 us
  waiting for transfers between devices  420 us (79%)
  matrix products  87.6 us (16%)
  between operations  13.6 us (3%)
  local copies, waits for them, and re-layouts  6.53 us (1%)
    all_gather x1, waiting for transfers between devices, local(): lax.all_gather(tokens, 'tensor', axis=1, tiled=True)  120 us
    all_gather x1, waiting for transfers between devices, local(): lax.all_gather(cotangent, 'tensor', axis=1, tiled=True)  100 us
    psum x1, waiting for transfers between devices, local(): summed = lax.psum(stacked, 'tensor')  72.4 us
    all_gather x1, waiting for transfers between devices, local(): lax.all_gather(gate_weight, 'dp', axis=0, tiled=True)  50.4 us
    all_gather x1, waiting for transfers between devices, local(): lax.all_gather(down_weight, 'dp', axis=1, tiled=True)  50.2 us
    dot_general x1, matrix products, local(): jnp.dot(columns, lax.all_gather(gate_weight, 'dp', axis=0, tiled=True), p...  26.2 us
    all_gather x1, waiting for transfers between devices, local(): lax.all_gather(up_weight, 'dp', axis=0, tiled=True)  23.4 us
    dot_general x1, matrix products, local(): lax.dot_general(columns, lax.all_gather(down_weight, 'dp', axis=1, tiled=...  22.8 us
  transfers between devices with their start and end apart: 6, of which 6 were waited for; matrix products, arithmetic and copies ran while one was open for 10% of the time, Pallas kernels for 0%

commit v1 on v0

v1 whole, which is shorter than its diff:
```python
import functools

import jax
import jax.numpy as jnp
from jax import lax
from jax.experimental import pallas as pl
from jax.experimental.pallas import tpu as pltpu
from jax.sharding import PartitionSpec as P

RANK = 64
DOCS = 8
PIECES = 4
MESH = pl.DeviceIdType.MESH


def outer_sums(onehot, left, right):
    weighted = (onehot[:, :, None] * left[:, None, :]).reshape(left.shape[0], -1)
    block = lax.dot_general(
        weighted,
        right,
        (((0,), (0,)), ((), ())),
        precision=lax.Precision.HIGHEST,
        preferred_element_type=jnp.float32,
    )
    return block.reshape(onehot.shape[1], -1)


def group_factors(projected, doc_rows):
    onehot = (doc_rows[:, None] == jnp.arange(DOCS, dtype=jnp.int32)[None, :]).astype(jnp.float32)
    p_tokens = projected[:, 0:RANK]
    p_cotan = projected[:, RANK : 2 * RANK]
    p_gate = projected[:, 2 * RANK : 3 * RANK]
    p_upgrad = projected[:, 3 * RANK : 4 * RANK]
    p_hidden = projected[:, 4 * RANK : 5 * RANK]
    return jnp.concatenate(
        [
            outer_sums(onehot, p_gate, p_tokens),
            outer_sums(onehot, p_upgrad, p_tokens),
            outer_sums(onehot, p_cotan, p_hidden),
        ],
        axis=1,
    )


def kernel(
    tensor, rows, feats, units, tile,
    tok_ref, cot_ref, gw_ref, uw_ref, dw_ref, ph_ref, pgate_ref, pup_ref, xpg_ref,
    out_ref,
    got, acc_g, acc_u, acc_h, swapped, gbuf, ubuf, dbuf, part, parts_in,
    swap_send, swap_recv, local_sem, z_up, z_down, z_recv, y_send, y_recv,
    w_sem, x_send, x_recv, x_free, rs_send, rs_recv, ag_send, ag_recv,
):
    n = tensor // 4
    planes = tensor // 2
    piece = rows * 2 // PIECES
    per_group = PIECES // 2
    tiles = units // tile
    own_rows = rows // tensor
    t = lax.axis_index("tensor")
    d = lax.axis_index("dp")
    z, y = t // 2, t % 2
    half = t // (2 * n)
    is_src = half == d
    own_blk = t - half * (2 * n)
    near = jnp.clip(z - d * n, 0, n - 1)

    def peer(k):
        return lax.rem(t + k, tensor)

    def column(i):
        return lax.rem(near - i + n, n)

    barrier = pltpu.get_barrier_semaphore()
    pl.semaphore_signal(barrier, inc=1, device_id={"dp": 1 - d}, device_id_type=MESH)
    for k in range(1, tensor):
        pl.semaphore_signal(barrier, inc=1, device_id={"tensor": peer(k)}, device_id_type=MESH)

    def w_gate(blk):
        return pltpu.make_async_copy(gw_ref.at[pl.ds(blk * feats, feats)], gbuf, w_sem.at[0])

    def w_up(blk):
        return pltpu.make_async_copy(uw_ref.at[pl.ds(blk * feats, feats)], ubuf, w_sem.at[1])

    def w_down(blk):
        at = pl.multiple_of(blk * feats, feats)
        return pltpu.make_async_copy(dw_ref.at[:, pl.ds(at, feats)], dbuf, w_sem.at[2])

    def blk_own(i):
        return column(i) * 2 + y

    def blk_cross(i):
        return column(i) * 2 + 1 - y

    w_gate(blk_own(0)).start()
    w_up(blk_own(0)).start()
    w_down(blk_own(0)).start()

    srcs = (tok_ref, cot_ref)

    def local(a):
        return pltpu.make_async_copy(srcs[a], got.at[a, own_blk, d], local_sem.at[a])

    def swap(a, group):
        return pltpu.make_async_remote_copy(
            src_ref=srcs[a], dst_ref=got.at[a, own_blk, group],
            send_sem=swap_send.at[a], recv_sem=swap_recv.at[a],
            device_id={"dp": 1 - d}, device_id_type=MESH,
        )

    @pl.when(is_src)
    def _():
        for a in range(2):
            local(a).start()

    pl.semaphore_wait(barrier, tensor)

    @pl.when(jnp.logical_not(is_src))
    def _():
        for a in range(2):
            swap(a, d).start()

    def where(a, c, yy, p):
        return got.at[a, c * 2 + yy, p // per_group, pl.ds((p % per_group) * piece, piece)]

    def sem_at(a, c, p):
        return (a * n + c) * PIECES + p

    def z_copy(a, c, p, up):
        ref = where(a, c, y, p)
        step = 2 if up else -2
        return pltpu.make_async_remote_copy(
            src_ref=ref, dst_ref=ref,
            send_sem=(z_up if up else z_down).at[sem_at(a, c, p)],
            recv_sem=z_recv.at[sem_at(a, c, p)],
            device_id={"tensor": lax.rem(t + step + tensor, tensor)}, device_id_type=MESH,
        )

    def y_copy(a, c, yy, p):
        ref = where(a, c, yy, p)
        return pltpu.make_async_remote_copy(
            src_ref=ref, dst_ref=ref,
            send_sem=y_send.at[sem_at(a, c, p)],
            recv_sem=y_recv.at[sem_at(a, c, p)],
            device_id={"tensor": t + 1 - 2 * y}, device_id_type=MESH,
        )

    def goes_up(c):
        return jnp.logical_and(z >= d * n + c, z < planes - 1)

    def goes_down(c):
        return jnp.logical_and(z <= d * n + c, z > 0)

    def comm(a, i, first):
        c = column(i)
        if first:
            @pl.when(is_src)
            def _():
                local(a).wait()
                swap(a, 1 - d).wait_recv()

        for p in range(PIECES):
            @pl.when(z != d * n + c)
            def _():
                z_copy(a, c, p, True).wait_recv()

            @pl.when(goes_up(c))
            def _():
                z_copy(a, c, p, True).start()

            @pl.when(goes_down(c))
            def _():
                z_copy(a, c, p, False).start()

            y_copy(a, c, y, p).start()

    def wait_cross(a, i):
        for p in range(PIECES):
            y_copy(a, column(i), 1 - y, p).wait_recv()

    def add_tokens(blk):
        def body(k, carry):
            g, j = k // tiles, k % tiles
            at = pl.ds(pl.multiple_of(j * tile, tile), tile)
            x = got[0, blk, g]
            acc_g[g, :, at] += jnp.dot(x, gbuf[:, at], preferred_element_type=jnp.float32)
            acc_u[g, :, at] += jnp.dot(x, ubuf[:, at], preferred_element_type=jnp.float32)
            return carry

        w_gate(blk).wait()
        w_up(blk).wait()
        lax.fori_loop(0, 2 * tiles, body, 0)

    def add_cotangent(blk):
        def body(k, carry):
            g, j = k // tiles, k % tiles
            start = pl.multiple_of(j * tile, tile)
            at = pl.ds(start, tile)
            acc_h[g, :, at] += lax.dot_general(
                got[1, blk, g], dbuf[at, :], (((1,), (1,)), ((), ())),
                preferred_element_type=jnp.float32,
            )
            return carry

        w_down(blk).wait()
        lax.fori_loop(0, 2 * tiles, body, 0)

    def next_tokens(blk):
        w_gate(blk).start()
        w_up(blk).start()

    def clear(j, carry):
        at = pl.ds(pl.multiple_of(j * tile, tile), tile)
        for g in range(2):
            zero = jnp.zeros((rows, tile), jnp.float32)
            acc_g[g, :, at] = zero
            acc_u[g, :, at] = zero
            acc_h[g, :, at] = zero
        return carry

    lax.fori_loop(0, tiles, clear, 0)
    part[:, 0:128] = xpg_ref[...]
    part[:, 128:384] = jnp.zeros((rows, 256), jnp.float32)

    def exchange(k):
        return pltpu.make_async_remote_copy(
            src_ref=(acc_g, acc_u, acc_h)[k].at[1 - d], dst_ref=swapped.at[k % 2],
            send_sem=x_send.at[k], recv_sem=x_recv.at[k],
            device_id={"dp": 1 - d}, device_id_type=MESH,
        )

    comm(0, 0, True)
    add_tokens(blk_own(0))

    def token_step(i, carry):
        next_tokens(blk_own(i))
        comm(0, i, False)
        add_tokens(blk_own(i))
        next_tokens(blk_cross(i - 1))
        wait_cross(0, i - 1)
        add_tokens(blk_cross(i - 1))
        return carry

    lax.fori_loop(1, n, token_step, 0)
    next_tokens(blk_cross(n - 1))

    comm(1, 0, True)
    add_cotangent(blk_own(0))
    wait_cross(0, n - 1)
    add_tokens(blk_cross(n - 1))
    exchange(0).start()
    exchange(1).start()

    def cotangent_step(i, carry):
        w_down(blk_own(i)).start()
        comm(1, i, False)
        add_cotangent(blk_own(i))
        w_down(blk_cross(i - 1)).start()
        wait_cross(1, i - 1)
        add_cotangent(blk_cross(i - 1))
        return carry

    lax.fori_loop(1, n, cotangent_step, 0)
    w_down(blk_cross(n - 1)).start()

    exchange(0).wait_recv()
    exchange(1).wait_recv()

    def activate(j, carry):
        at = pl.ds(pl.multiple_of(j * tile, tile), tile)
        gate = acc_g[d, :, at] + swapped[0, :, at]
        up = acc_u[d, :, at] + swapped[1, :, at]
        s = jax.nn.sigmoid(gate)
        silu = gate * s
        acc_g[d, :, at] = silu
        acc_u[d, :, at] = up * s * (1.0 + gate * (1.0 - s))
        hidden = (silu * up).astype(jnp.bfloat16)
        part[:, 256:384] += jnp.dot(hidden, ph_ref[at, :], preferred_element_type=jnp.float32)
        return carry

    lax.fori_loop(0, tiles, activate, 0)
    pl.semaphore_signal(x_free, inc=1, device_id={"dp": 1 - d}, device_id_type=MESH)

    wait_cross(1, n - 1)
    add_cotangent(blk_cross(n - 1))
    pl.semaphore_wait(x_free, 1)
    exchange(2).start()
    exchange(2).wait_recv()

    def gradients(j, carry):
        at = pl.ds(pl.multiple_of(j * tile, tile), tile)
        grad = acc_h[d, :, at] + swapped[0, :, at]
        grad_up = (grad * acc_g[d, :, at]).astype(jnp.bfloat16)
        grad_gate = (grad * acc_u[d, :, at]).astype(jnp.bfloat16)
        part[:, 128:256] += jnp.dot(
            grad_gate, pgate_ref[at, :], preferred_element_type=jnp.float32
        ) + jnp.dot(grad_up, pup_ref[at, :], preferred_element_type=jnp.float32)
        return carry

    lax.fori_loop(0, tiles, gradients, 0)

    def rs_copy(k):
        return pltpu.make_async_remote_copy(
            src_ref=part.at[pl.ds(pl.multiple_of(peer(k) * own_rows, own_rows), own_rows)],
            dst_ref=parts_in.at[k - 1],
            send_sem=rs_send.at[k - 1], recv_sem=rs_recv.at[k - 1],
            device_id={"tensor": peer(k)}, device_id_type=MESH,
        )

    def ag_copy(k, owner):
        ref = out_ref.at[pl.ds(pl.multiple_of(owner * own_rows, own_rows), own_rows)]
        return pltpu.make_async_remote_copy(
            src_ref=ref, dst_ref=ref,
            send_sem=ag_send.at[k - 1], recv_sem=ag_recv.at[k - 1],
            device_id={"tensor": peer(k)}, device_id_type=MESH,
        )

    mine = pl.ds(pl.multiple_of(t * own_rows, own_rows), own_rows)
    for k in range(1, tensor):
        rs_copy(k).start()
    total = part[mine, :]
    for k in range(1, tensor):
        rs_copy(k).wait_recv()
        total += parts_in[k - 1]
    out_ref[mine, :] = total
    for k in range(1, tensor):
        ag_copy(k, t).start()
    for k in range(1, tensor):
        ag_copy(k, peer(tensor - k)).wait_recv()

    for k in range(1, tensor):
        rs_copy(k).wait_send()
        ag_copy(k, t).wait_send()
    for k in range(3):
        exchange(k).wait_send()

    @pl.when(jnp.logical_not(is_src))
    def _():
        for a in range(2):
            swap(a, d).wait_send()

    def drain(c, carry):
        for a in range(2):
            for p in range(PIECES):
                @pl.when(goes_up(c))
                def _():
                    z_copy(a, c, p, True).wait_send()

                @pl.when(goes_down(c))
                def _():
                    z_copy(a, c, p, False).wait_send()

                y_copy(a, c, y, p).wait_send()
        return carry

    lax.fori_loop(0, n, drain, 0)


def projected_rows(tensor, tokens, cotangent, gate_weight, up_weight, down_weight, ph, pgate, pup, xpg):
    rows, feats = tokens.shape
    units = gate_weight.shape[1]
    tile = 256 if units % 256 == 0 else units
    n = tensor // 4
    steps = 2 * n * PIECES
    anywhere = pl.BlockSpec(memory_space=pl.ANY)
    vmem = pl.BlockSpec(memory_space=pltpu.VMEM)
    dma = pltpu.SemaphoreType.DMA
    f32, bf16 = jnp.float32, jnp.bfloat16
    return pl.pallas_call(
        functools.partial(kernel, tensor, rows, feats, units, tile),
        out_shape=jax.ShapeDtypeStruct((rows, 384), f32),
        in_specs=[anywhere] * 5 + [vmem] * 4,
        out_specs=vmem,
        scratch_shapes=[
            pltpu.VMEM((2, 2 * n, 2, rows, feats), bf16),
            pltpu.VMEM((2, rows, units), f32),
            pltpu.VMEM((2, rows, units), f32),
            pltpu.VMEM((2, rows, units), f32),
            pltpu.VMEM((2, rows, units), f32),
            pltpu.VMEM((feats, units), bf16),
            pltpu.VMEM((feats, units), bf16),
            pltpu.VMEM((units, feats), bf16),
            pltpu.VMEM((rows, 384), f32),
            pltpu.VMEM((tensor - 1, rows // tensor, 384), f32),
            dma((2,)), dma((2,)), dma((2,)),
            dma((steps,)), dma((steps,)), dma((steps,)), dma((steps,)), dma((steps,)),
            dma((3,)), dma((3,)), dma((3,)), pltpu.SemaphoreType.REGULAR,
            dma((tensor - 1,)), dma((tensor - 1,)), dma((tensor - 1,)), dma((tensor - 1,)),
        ],
        compiler_params=pltpu.CompilerParams(
            collective_id=0, has_side_effects=True, vmem_limit_bytes=61 * 1024 * 1024
        ),
    )(tokens, cotangent, gate_weight, up_weight, down_weight, ph, pgate, pup, xpg)


def local(
    tensor,
    tokens,
    cotangent,
    gate_weight,
    up_weight,
    down_weight,
    proj_tokens,
    proj_cotangent,
    proj_hidden,
    proj_gate,
    proj_up,
    doc_ids,
    query_grads,
):
    xpg = jnp.concatenate(
        [
            jnp.dot(tokens, proj_tokens, preferred_element_type=jnp.float32),
            jnp.dot(cotangent, proj_cotangent, preferred_element_type=jnp.float32),
        ],
        axis=1,
    )
    summed = projected_rows(
        tensor, tokens, cotangent, gate_weight, up_weight, down_weight,
        jnp.pad(proj_hidden, ((0, 0), (0, RANK))), jnp.pad(proj_gate, ((0, 0), (0, RANK))),
        jnp.pad(proj_up, ((0, 0), (RANK, 0))), xpg,
    )
    factors = group_factors(summed, doc_ids[0])
    return jnp.dot(
        factors,
        query_grads.astype(jnp.float32).T,
        precision=lax.Precision.HIGHEST,
        preferred_element_type=jnp.float32,
    )


def solution(mesh):
    return jax.shard_map(
        functools.partial(local, mesh.shape["tensor"]),
        mesh=mesh,
        in_specs=(
            P(("parts", "dp"), "tensor"),
            P(("parts", "dp"), "tensor"),
            P("dp", "tensor"),
            P("dp", "tensor"),
            P("tensor", "dp"),
            P("tensor", None),
            P("tensor", None),
            P("tensor", None),
            P("tensor", None),
            P("tensor", None),
            P(("parts", "dp"), None),
            P("tensor", None),
        ),
        out_specs=P(("parts", "dp"), "tensor"),
        check_vma=False,
    )
```

time: 532 us -> 262 us (0.49)
  waiting for transfers between devices: 420 us -> 0 us
  Pallas kernels: 0 us -> 236 us
  matrix products: 87.6 us -> 11.3 us
  between operations: 13.6 us -> 0.07 us
    all_gather x5 -> x0, waiting for transfers between devices: 344 us -> none  [the longest x1 120 us: local(): lax.all_gather(tokens, 'tensor', axis=1, tiled=True)]
    pallas_call x0 -> x1, Pallas kernels: none -> 236 us  [projected_rows(): pl.pallas_call(functools.partial(kernel, tensor, rows, feats, units, tile...]
    dot_general x6 -> x0, matrix products: 78.5 us -> none  [the longest x1 26.2 us: local(): jnp.dot(columns, lax.all_gather(gate_weight, 'dp', axis=0, tiled=True), p...]
    psum x1 -> x0, waiting for transfers between devices: 72.4 us -> none  [local(): summed = lax.psum(stacked, 'tensor')]
  transfers between devices with their start and end apart: 6 -> 0, of which waited for: 6 -> 0; matrix products, arithmetic and copies ran while one was open for 10% -> 0% of each run, Pallas kernels for 0% -> 0%
where the time goes in v1:
time: 262 us; the launch traced here: 261 us
  Pallas kernels  236 us (90%)
  matrix products  11.3 us (4%)
  local copies, waits for them, and re-layouts  9.77 us (4%)
  other arithmetic  4.02 us (2%)
    pallas_call x1, Pallas kernels, projected_rows(): pl.pallas_call(functools.partial(kernel, tensor, rows, feats, units, tile...  236 us
    dot_general x3, matrix products, outer_sums(): lax.dot_general(weighted, right, (((0,), (0,)), ((), ())), precision=lax....  6.28 us

profile of v1, /device:TPU:13, one launch (start us, length us, event | category | flops | bytes accessed | tf_op | source)
XLA Modules:
  0.0 261.0 jit_solution(13311896635524982898)
XLA Ops:
  0.0 0.0 copy-start
  0.0 0.0 copy-start.2
  0.0 0.8 fusion.12
  0.8 1.7 fusion.15
  2.5 0.0 copy-done.2
  2.5 0.0 copy-start.4
  2.6 1.4 fusion.16
  3.9 0.8 pad_maximum_fusion.xpg_ref
  4.8 0.0 copy-done.3
  4.8 0.3 copy.18
  5.0 0.9 pad.11.ph_ref
  5.9 0.0 copy-done.4
  5.9 0.3 copy.19
  6.2 0.9 pad.12.pgate_ref
  7.1 0.0 copy-done.5
  7.1 0.3 copy.20
  7.4 1.0 pad.13.pup_ref
  8.3 235.9 %shard_map.118 = f32[512,384]{1,0:T(8,128)} custom-call(bf16[512,1024]{1,0:T(8,128)(2,1)} %tok_ref.1, bf16[512,1024]{1,0:T(8,128)(2,1)} %cot_ref.1, bf16[4096,1792]{1,0:T(8,128)(2,1)} %gw_ref.1, bf16[4096,1792]{1,0:T(8,128)(2,1)} %uw_ref.1, bf16[1792,4096]{1,0:T(8,128)(2,1)} %dw_ref.1, bf16[1792,128]{1,0:T(8,128)(2,1)} %pad.11.ph_ref, ...), custom_call_target="tpu_custom_call" | custom-call | tf_op jit(solution)/shard_map/pallas_call | solution.py:368
  244.2 1.3 fusion.14
  245.5 0.1 copy.23
  245.7 0.8 copy.27
  246.4 0.8 copy.25
  247.2 2.3 broadcast_multiply_fusion.2
  249.6 0.0 copy-done.1
  249.6 1.7 fusion.10
  251.3 1.1 reshape.49
  252.3 2.9 %fusion.8 = f32[512,64]{1,0:T(8,128)} fusion(f32[512,512]{0,1:T(8,128)} %bitcast.13, f32[512,384]{1,0:T(8,128)S(1)} %copy-done.1), kind=kOutput, calls=%fused_computation.12 | convolution fusion | flops 201326592 | bytes 1441792 | tf_op jit(solution)/shard_map/dot_general | solution.py:18
  255.2 1.7 fusion.6
  256.9 1.1 reshape.51
  258.0 1.1 reshape.50
  259.0 0.0 copy-done
  259.1 1.9 fusion
  (3 shorter events, 0.0 us)
Async XLA Ops:
  0.0 259.0 %copy-start = (bf16[64,12288]{1,0:T(8,128)(2,1)S(1)}, bf16[64,12288]{1,0:T(8,128)(2,1)}, u32[]{:S(2)}) copy-start(bf16[64,12288]{1,0:T(8,128)(2,1)} %param.23) | copy-start | bytes 4718596
  0.0 2.5 copy-start.2
  0.8 3.9 %copy-start.3 = (bf16[1792,64]{0,1:T(8,128)(2,1)S(1)}, bf16[1792,64]{0,1:T(8,128)(2,1)}, u32[]{:S(2)}) copy-start(bf16[1792,64]{0,1:T(8,128)(2,1)} %param.19) | copy-start | bytes 688132
  2.5 3.4 %copy-start.4 = (bf16[1792,64]{0,1:T(8,128)(2,1)S(1)}, bf16[1792,64]{0,1:T(8,128)(2,1)}, u32[]{:S(2)}) copy-start(bf16[1792,64]{0,1:T(8,128)(2,1)} %param.20) | copy-start | bytes 688132
  4.8 2.3 copy-start.5
  247.2 2.4 copy-start.1

commit v2 on v1

--- a/solution.py
+++ b/solution.py
@@ -47,7 +47,7 @@
     tok_ref, cot_ref, gw_ref, uw_ref, dw_ref, ph_ref, pgate_ref, pup_ref, xpg_ref,
     out_ref,
     got, acc_g, acc_u, acc_h, swapped, gbuf, ubuf, dbuf, part, parts_in,
-    swap_send, swap_recv, local_sem, z_up, z_down, z_recv, y_send, y_recv,
+    swap_send, swap_recv, local_sem, z_up, z_down, z_recv, y_send, y_recv, s_send, s_recv,
     w_sem, x_send, x_recv, x_free, rs_send, rs_recv, ag_send, ag_recv,
 ):
     n = tensor // 4
@@ -171,11 +171,46 @@
             def _():
                 z_copy(a, c, p, False).start()
 
-            y_copy(a, c, y, p).start()
+            if p < PIECES // 2:
+                y_copy(a, c, y, p).start()
+            else:
+                @pl.when(crosses(c))
+                def _():
+                    y_copy(a, c, y, p).start()
+
+    end_c = d * (n - 1)
+    end_z = d * (planes - 1)
+    last_z = (planes - 1) - end_z
+
+    def crosses(c):
+        return jnp.logical_or(c != end_c, z == end_z)
+
+    def side_copy(a, p):
+        ref = where(a, end_c, 1 - y, p)
+        to = jnp.clip(t + 2 - 4 * d, 0, tensor - 1)
+        q = a * (PIECES // 2) + p - PIECES // 2
+        return pltpu.make_async_remote_copy(
+            src_ref=ref, dst_ref=ref, send_sem=s_send.at[q], recv_sem=s_recv.at[q],
+            device_id={"tensor": to}, device_id_type=MESH,
+        )
 
     def wait_cross(a, i):
-        for p in range(PIECES):
-            y_copy(a, column(i), 1 - y, p).wait_recv()
+        c = column(i)
+        for p in range(PIECES // 2, PIECES):
+            @pl.when(crosses(c))
+            def _():
+                y_copy(a, c, 1 - y, p).wait_recv()
+
+            @pl.when(jnp.logical_not(crosses(c)))
+            def _():
+                side_copy(a, p).wait_recv()
+
+            @pl.when(jnp.logical_and(c == end_c, z != last_z))
+            def _():
+                side_copy(a, p).start()
+
+        for p in range(PIECES // 2):
+            y_copy(a, c, 1 - y, p).wait_recv()
 
     def add_tokens(blk):
         def body(k, carry):
@@ -349,10 +384,21 @@
                 def _():
                     z_copy(a, c, p, False).wait_send()
 
-                y_copy(a, c, y, p).wait_send()
+                if p < PIECES // 2:
+                    y_copy(a, c, y, p).wait_send()
+                else:
+                    @pl.when(crosses(c))
+                    def _():
+                        y_copy(a, c, y, p).wait_send()
         return carry
 
     lax.fori_loop(0, n, drain, 0)
+
+    @pl.when(z != last_z)
+    def _():
+        for a in range(2):
+            for p in range(PIECES // 2, PIECES):
+                side_copy(a, p).wait_send()
 
 
 def projected_rows(tensor, tokens, cotangent, gate_weight, up_weight, down_weight, ph, pgate, pup, xpg):
@@ -383,6 +429,7 @@
             pltpu.VMEM((tensor - 1, rows // tensor, 384), f32),
             dma((2,)), dma((2,)), dma((2,)),
             dma((steps,)), dma((steps,)), dma((steps,)), dma((steps,)), dma((steps,)),
+            dma((PIECES,)), dma((PIECES,)),
             dma((3,)), dma((3,)), dma((3,)), pltpu.SemaphoreType.REGULAR,
             dma((tensor - 1,)), dma((tensor - 1,)), dma((tensor - 1,)), dma((tensor - 1,)),
         ],

time: 262 us -> 241 us (0.920)
  Pallas kernels: 236 us -> 216 us
    pallas_call x1, Pallas kernels: 236 us -> 216 us  [projected_rows(): pl.pallas_call(functools.partial(kernel, tensor, rows, feats, units, tile...]
where the time goes in v2:
time: 241 us
  Pallas kernels  216 us (90%)
  matrix products  11.3 us (5%)
  local copies, waits for them, and re-layouts  9.77 us (4%)
  other arithmetic  4.02 us (2%)
    pallas_call x1, Pallas kernels, projected_rows(): pl.pallas_call(functools.partial(kernel, tensor, rows, feats, units, tile...  216 us
    dot_general x3, matrix products, outer_sums(): lax.dot_general(weighted, right, (((0,), (0,)), ((), ())), precision=lax....  6.28 us

profile of v2, /device:TPU:13, one launch (start us, length us, event | category | flops | bytes accessed | tf_op | source)
XLA Modules:
  0.0 240.8 jit_solution(14452000946149260690)
XLA Ops:
  0.0 0.0 copy-start
  0.0 0.0 copy-start.2
  0.0 0.8 fusion.12
  0.8 1.7 fusion.15
  2.5 0.0 copy-done.2
  2.5 0.0 copy-start.4
  2.6 1.4 fusion.16
  3.9 0.8 pad_maximum_fusion.xpg_ref
  4.8 0.0 copy-done.3
  4.8 0.3 copy.18
  5.0 0.9 pad.11.ph_ref
  5.9 0.0 copy-done.4
  5.9 0.3 copy.19
  6.2 0.9 pad.12.pgate_ref
  7.1 0.0 copy-done.5
  7.1 0.3 copy.20
  7.4 1.0 pad.13.pup_ref
  8.3 215.7 %shard_map.118 = f32[512,384]{1,0:T(8,128)} custom-call(bf16[512,1024]{1,0:T(8,128)(2,1)} %tok_ref.1, bf16[512,1024]{1,0:T(8,128)(2,1)} %cot_ref.1, bf16[4096,1792]{1,0:T(8,128)(2,1)} %gw_ref.1, bf16[4096,1792]{1,0:T(8,128)(2,1)} %uw_ref.1, bf16[1792,4096]{1,0:T(8,128)(2,1)} %dw_ref.1, bf16[1792,128]{1,0:T(8,128)(2,1)} %pad.11.ph_ref, ...), custom_call_target="tpu_custom_call" | custom-call | tf_op jit(solution)/shard_map/pallas_call | solution.py:414
  224.1 1.3 fusion.14
  225.4 0.1 copy.23
  225.5 0.8 copy.27
  226.3 0.8 copy.25
  227.1 2.3 broadcast_multiply_fusion.2
  229.4 0.0 copy-done.1
  229.4 1.7 fusion.10
  231.1 1.1 reshape.49
  232.2 2.9 %fusion.8 = f32[512,64]{1,0:T(8,128)} fusion(f32[512,512]{0,1:T(8,128)} %bitcast.13, f32[512,384]{1,0:T(8,128)S(1)} %copy-done.1), kind=kOutput, calls=%fused_computation.12 | convolution fusion | flops 201326592 | bytes 1441792 | tf_op jit(solution)/shard_map/dot_general | solution.py:18
  235.1 1.7 fusion.6
  236.8 1.1 reshape.51
  237.8 1.1 reshape.50
  238.9 0.0 copy-done
  238.9 1.9 fusion
  (3 shorter events, 0.0 us)
Async XLA Ops:
  0.0 238.9 %copy-start = (bf16[64,12288]{1,0:T(8,128)(2,1)S(1)}, bf16[64,12288]{1,0:T(8,128)(2,1)}, u32[]{:S(2)}) copy-start(bf16[64,12288]{1,0:T(8,128)(2,1)} %param.23) | copy-start | bytes 4718596
  0.0 2.5 %copy-start.2 = (bf16[512,1024]{1,0:T(8,128)(2,1)S(1)}, bf16[512,1024]{1,0:T(8,128)(2,1)}, u32[]{:S(2)}) copy-start(bf16[512,1024]{1,0:T(8,128)(2,1)} %cot_ref.1) | copy-start | bytes 3145732
  0.8 3.9 %copy-start.3 = (bf16[1792,64]{0,1:T(8,128)(2,1)S(1)}, bf16[1792,64]{0,1:T(8,128)(2,1)}, u32[]{:S(2)}) copy-start(bf16[1792,64]{0,1:T(8,128)(2,1)} %param.19) | copy-start | bytes 688132
  2.5 3.4 %copy-start.4 = (bf16[1792,64]{0,1:T(8,128)(2,1)S(1)}, bf16[1792,64]{0,1:T(8,128)(2,1)}, u32[]{:S(2)}) copy-start(bf16[1792,64]{0,1:T(8,128)(2,1)} %param.20) | copy-start | bytes 688132
  4.8 2.3 copy-start.5
  227.1 2.4 copy-start.1

commit v3 on v2

--- a/solution.py
+++ b/solution.py
@@ -44,9 +44,10 @@
 
 def kernel(
     tensor, rows, feats, units, tile,
-    tok_ref, cot_ref, gw_ref, uw_ref, dw_ref, ph_ref, pgate_ref, pup_ref, xpg_ref,
+    tok_ref, cot_ref, gw_ref, uw_ref, dw_ref, pt_in, pc_in, ph_in, pgate_in, pup_in,
     out_ref,
-    got, acc_g, acc_u, acc_h, swapped, gbuf, ubuf, dbuf, part, parts_in,
+    got, acc_g, acc_u, acc_h, swapped, gbuf, dbuf, part, parts_in,
+    xbuf, pt_ref, pc_ref, ph_ref, pgate_ref, pup_ref, in_sem,
     swap_send, swap_recv, local_sem, z_up, z_down, z_recv, y_send, y_recv, s_send, s_recv,
     w_sem, x_send, x_recv, x_free, rs_send, rs_recv, ag_send, ag_recv,
 ):
@@ -79,7 +80,7 @@
         return pltpu.make_async_copy(gw_ref.at[pl.ds(blk * feats, feats)], gbuf, w_sem.at[0])
 
     def w_up(blk):
-        return pltpu.make_async_copy(uw_ref.at[pl.ds(blk * feats, feats)], ubuf, w_sem.at[1])
+        return pltpu.make_async_copy(uw_ref.at[pl.ds(blk * feats, feats)], gbuf, w_sem.at[1])
 
     def w_down(blk):
         at = pl.multiple_of(blk * feats, feats)
@@ -92,10 +93,22 @@
         return column(i) * 2 + 1 - y
 
     w_gate(blk_own(0)).start()
-    w_up(blk_own(0)).start()
     w_down(blk_own(0)).start()
 
     srcs = (tok_ref, cot_ref)
+    projections = (
+        (pt_in, pt_ref), (pc_in, pc_ref), (ph_in, ph_ref), (pgate_in, pgate_ref), (pup_in, pup_ref)
+    )
+
+    def load(k):
+        return pltpu.make_async_copy(projections[k][0], projections[k][1], in_sem.at[k])
+
+    def own_rows_in(a):
+        return pltpu.make_async_copy(srcs[a], xbuf, in_sem.at[5 + a])
+
+    for k in range(5):
+        load(k).start()
+    own_rows_in(0).start()
 
     def local(a):
         return pltpu.make_async_copy(srcs[a], got.at[a, own_blk, d], local_sem.at[a])
@@ -213,17 +226,22 @@
             y_copy(a, c, 1 - y, p).wait_recv()
 
     def add_tokens(blk):
-        def body(k, carry):
-            g, j = k // tiles, k % tiles
-            at = pl.ds(pl.multiple_of(j * tile, tile), tile)
-            x = got[0, blk, g]
-            acc_g[g, :, at] += jnp.dot(x, gbuf[:, at], preferred_element_type=jnp.float32)
-            acc_u[g, :, at] += jnp.dot(x, ubuf[:, at], preferred_element_type=jnp.float32)
-            return carry
+        def add_into(acc):
+            def body(k, carry):
+                g, j = k // tiles, k % tiles
+                at = pl.ds(pl.multiple_of(j * tile, tile), tile)
+                acc[g, :, at] += jnp.dot(
+                    got[0, blk, g], gbuf[:, at], preferred_element_type=jnp.float32
+                )
+                return carry
+
+            lax.fori_loop(0, 2 * tiles, body, 0)
 
         w_gate(blk).wait()
+        add_into(acc_g)
+        w_up(blk).start()
         w_up(blk).wait()
-        lax.fori_loop(0, 2 * tiles, body, 0)
+        add_into(acc_u)
 
     def add_cotangent(blk):
         def body(k, carry):
@@ -241,7 +259,6 @@
 
     def next_tokens(blk):
         w_gate(blk).start()
-        w_up(blk).start()
 
     def clear(j, carry):
         at = pl.ds(pl.multiple_of(j * tile, tile), tile)
@@ -253,8 +270,7 @@
         return carry
 
     lax.fori_loop(0, tiles, clear, 0)
-    part[:, 0:128] = xpg_ref[...]
-    part[:, 128:384] = jnp.zeros((rows, 256), jnp.float32)
+    part[...] = jnp.zeros_like(part)
 
     def exchange(k):
         return pltpu.make_async_remote_copy(
@@ -264,7 +280,16 @@
         )
 
     comm(0, 0, True)
+    for k in range(5):
+        load(k).wait()
+    own_rows_in(0).wait()
+    px = jnp.dot(xbuf[...], pt_ref[...], preferred_element_type=jnp.float32)
+    part[:, 0:128] = jnp.concatenate([px, jnp.zeros_like(px)], axis=1)
+    own_rows_in(1).start()
     add_tokens(blk_own(0))
+    own_rows_in(1).wait()
+    pg = jnp.dot(xbuf[...], pc_ref[...], preferred_element_type=jnp.float32)
+    part[:, 0:128] += jnp.concatenate([jnp.zeros_like(pg), pg], axis=1)
 
     def token_step(i, carry):
         next_tokens(blk_own(i))
@@ -309,7 +334,9 @@
         acc_g[d, :, at] = silu
         acc_u[d, :, at] = up * s * (1.0 + gate * (1.0 - s))
         hidden = (silu * up).astype(jnp.bfloat16)
-        part[:, 256:384] += jnp.dot(hidden, ph_ref[at, :], preferred_element_type=jnp.float32)
+        part[:, 256 : 256 + RANK] += jnp.dot(
+            hidden, ph_ref[at, :], preferred_element_type=jnp.float32
+        )
         return carry
 
     lax.fori_loop(0, tiles, activate, 0)
@@ -326,9 +353,13 @@
         grad = acc_h[d, :, at] + swapped[0, :, at]
         grad_up = (grad * acc_g[d, :, at]).astype(jnp.bfloat16)
         grad_gate = (grad * acc_u[d, :, at]).astype(jnp.bfloat16)
-        part[:, 128:256] += jnp.dot(
-            grad_gate, pgate_ref[at, :], preferred_element_type=jnp.float32
-        ) + jnp.dot(grad_up, pup_ref[at, :], preferred_element_type=jnp.float32)
+        part[:, 128:256] += jnp.concatenate(
+            [
+                jnp.dot(grad_gate, pgate_ref[at, :], preferred_element_type=jnp.float32),
+                jnp.dot(grad_up, pup_ref[at, :], preferred_element_type=jnp.float32),
+            ],
+            axis=1,
+        )
         return carry
 
     lax.fori_loop(0, tiles, gradients, 0)
@@ -401,7 +432,7 @@
                 side_copy(a, p).wait_send()
 
 
-def projected_rows(tensor, tokens, cotangent, gate_weight, up_weight, down_weight, ph, pgate, pup, xpg):
+def projected_rows(tensor, tokens, cotangent, gate_weight, up_weight, down_weight, pt, pc, ph, pgate, pup):
     rows, feats = tokens.shape
     units = gate_weight.shape[1]
     tile = 256 if units % 256 == 0 else units
@@ -414,7 +445,7 @@
     return pl.pallas_call(
         functools.partial(kernel, tensor, rows, feats, units, tile),
         out_shape=jax.ShapeDtypeStruct((rows, 384), f32),
-        in_specs=[anywhere] * 5 + [vmem] * 4,
+        in_specs=[anywhere] * 10,
         out_specs=vmem,
         scratch_shapes=[
             pltpu.VMEM((2, 2 * n, 2, rows, feats), bf16),
@@ -423,10 +454,16 @@
             pltpu.VMEM((2, rows, units), f32),
             pltpu.VMEM((2, rows, units), f32),
             pltpu.VMEM((feats, units), bf16),
-            pltpu.VMEM((feats, units), bf16),
             pltpu.VMEM((units, feats), bf16),
             pltpu.VMEM((rows, 384), f32),
             pltpu.VMEM((tensor - 1, rows // tensor, 384), f32),
+            pltpu.VMEM((rows, feats), bf16),
+            pltpu.VMEM((feats, RANK), bf16),
+            pltpu.VMEM((feats, RANK), bf16),
+            pltpu.VMEM((units, RANK), bf16),
+            pltpu.VMEM((units, RANK), bf16),
+            pltpu.VMEM((units, RANK), bf16),
+            dma((7,)),
             dma((2,)), dma((2,)), dma((2,)),
             dma((steps,)), dma((steps,)), dma((steps,)), dma((steps,)), dma((steps,)),
             dma((PIECES,)), dma((PIECES,)),
@@ -436,7 +473,7 @@
         compiler_params=pltpu.CompilerParams(
             collective_id=0, has_side_effects=True, vmem_limit_bytes=61 * 1024 * 1024
         ),
-    )(tokens, cotangent, gate_weight, up_weight, down_weight, ph, pgate, pup, xpg)
+    )(tokens, cotangent, gate_weight, up_weight, down_weight, pt, pc, ph, pgate, pup)
 
 
 def local(
@@ -454,17 +491,9 @@
     doc_ids,
     query_grads,
 ):
-    xpg = jnp.concatenate(
-        [
-            jnp.dot(tokens, proj_tokens, preferred_element_type=jnp.float32),
-            jnp.dot(cotangent, proj_cotangent, preferred_element_type=jnp.float32),
-        ],
-        axis=1,
-    )
     summed = projected_rows(
         tensor, tokens, cotangent, gate_weight, up_weight, down_weight,
-        jnp.pad(proj_hidden, ((0, 0), (0, RANK))), jnp.pad(proj_gate, ((0, 0), (0, RANK))),
-        jnp.pad(proj_up, ((0, 0), (RANK, 0))), xpg,
+        proj_tokens, proj_cotangent, proj_hidden, proj_gate, proj_up,
     )
     factors = group_factors(summed, doc_ids[0])
     return jnp.dot(

time: 241 us -> 240 us (level)
  local copies, waits for them, and re-layouts: 9.77 us -> 13.7 us
  matrix products: 11.3 us -> 8.2 us
    unnamed x15 -> x13, local copies, waits for them, and re-layouts: 0.83 us -> 7.41 us
    dot_general x2 -> x0, matrix products: 3.05 us -> none  [the longest x1 1.69 us: local(): jnp.dot(tokens, proj_tokens, preferred_element_type=jnp.float32)]
    pad x3 -> x0, local copies, waits for them, and re-layouts: 2.75 us -> none  [the longest x1 0.98 us: local(): jnp.pad(proj_up, ((0, 0), (RANK, 0)))]
where the time goes in v3:
time: 240 us
  Pallas kernels  215 us (90%)
  local copies, waits for them, and re-layouts  13.7 us (6%)
  matrix products  8.2 us (3%)
  other arithmetic  3.17 us (1%)
    pallas_call x1, Pallas kernels, projected_rows(): pl.pallas_call(functools.partial(kernel, tensor, rows, feats, units, tile...  215 us
    unnamed x13, local copies, waits for them, and re-layouts  7.41 us
    dot_general x3, matrix products, outer_sums(): lax.dot_general(weighted, right, (((0,), (0,)), ((), ())), precision=lax....  6.27 us

profile of v3, /device:TPU:13, one launch (start us, length us, event | category | flops | bytes accessed | tf_op | source)
XLA Modules:
  0.0 239.8 jit_solution(6529218087784236981)
XLA Ops:
  0.0 0.0 copy-start
  0.0 0.0 copy-start.3
  0.0 0.0 copy-start.2
  0.0 0.8 fusion.12
  0.8 1.7 copy.18.pt_in
  2.6 1.7 copy.19.pc_in
  4.3 1.9 copy.20.ph_in
  6.3 0.0 copy-done.2
  6.3 1.0 copy.21.pgate_in
  7.3 0.0 copy-done.3
  7.3 1.0 copy.22.pup_in
  8.2 214.8 %shard_map.118 = f32[512,384]{1,0:T(8,128)} custom-call(bf16[512,1024]{1,0:T(8,128)(2,1)} %tok_ref.1, bf16[512,1024]{1,0:T(8,128)(2,1)} %cot_ref.1, bf16[4096,1792]{1,0:T(8,128)(2,1)} %gw_ref.1, bf16[4096,1792]{1,0:T(8,128)(2,1)} %uw_ref.1, bf16[1792,4096]{1,0:T(8,128)(2,1)} %dw_ref.1, bf16[1024,64]{1,0:T(8,128)(2,1)} %copy.18.pt_in, ...), custom_call_target="tpu_custom_call" | custom-call | tf_op jit(solution)/shard_map/pallas_call | solution.py:445
  223.0 1.4 fusion.14
  224.4 0.1 copy.23
  224.6 0.8 copy.27
  225.3 0.8 copy.25
  226.1 0.0 copy-start.1
  226.1 2.3 broadcast_multiply_fusion.2
  228.4 0.0 copy-done.1
  228.4 1.7 fusion.10
  230.1 1.1 reshape.49
  231.2 2.9 %fusion.8 = f32[512,64]{1,0:T(8,128)} fusion(f32[512,512]{0,1:T(8,128)} %bitcast.9, f32[512,384]{1,0:T(8,128)S(1)} %copy-done.1), kind=kOutput, calls=%fused_computation.11 | convolution fusion | flops 201326592 | bytes 1441792 | tf_op jit(solution)/shard_map/dot_general | solution.py:18
  234.1 1.7 fusion.6
  235.8 1.1 reshape.51
  236.8 1.1 reshape.50
  237.9 0.0 copy-done
  237.9 1.9 fusion
Async XLA Ops:
  0.0 237.9 %copy-start = (bf16[64,12288]{1,0:T(8,128)(2,1)S(1)}, bf16[64,12288]{1,0:T(8,128)(2,1)}, u32[]{:S(2)}) copy-start(bf16[64,12288]{1,0:T(8,128)(2,1)} %param.23) | copy-start | bytes 4718596
  0.0 7.3 %copy-start.3 = (bf16[1792,64]{0,1:T(8,128)(2,1)S(1)}, bf16[1792,64]{0,1:T(8,128)(2,1)}, u32[]{:S(2)}) copy-start(bf16[1792,64]{0,1:T(8,128)(2,1)} %param.21) | copy-start | bytes 688132
  0.0 6.3 %copy-start.2 = (bf16[1792,64]{0,1:T(8,128)(2,1)S(1)}, bf16[1792,64]{0,1:T(8,128)(2,1)}, u32[]{:S(2)}) copy-start(bf16[1792,64]{0,1:T(8,128)(2,1)} %param.20) | copy-start | bytes 688132
  226.1 2.3 copy-start.1
